TPU v7x, 256 devices: a whole 4x4x8 slice. The times are simulated.
256 devices in a mesh: blk: 16 (over z, y_lo), grp: 16 (over x, y_hi, core).
Axes of the slice: x: 4, y: 4 (y_hi: 2, y_lo: 2; y = y_hi * 2 + y_lo), z: 8, core: 2. Of those that a mesh axis runs over, the one named last changes fastest.
Arguments:
- state: float32 [2, 128, 32768], P(None, None, ('blk', 'grp')), may hold values from -3 to 3
- prev_slope: float32 [2, 128, 32768], P(None, None, ('blk', 'grp')), may hold values from -4 to 4
- positions: float32 [2, 32768], P(None, ('blk', 'grp')), may hold values from -1 to 1
- pump: float32 [32768], P(('blk', 'grp')), may hold values from -0.5 to 1.5
- detuning: float32 [32768], P(('blk', 'grp')), may hold values from -4 to 4
- kappa: float32 [6, 32768], P(None, ('blk', 'grp')), may hold values from 0.2 to 1
- neighbours: int32 [6, 32768], P(None, ('blk', 'grp')), may hold values from 0 to 255
- send_list: int32 [2, 16384], P(None, ('blk', 'grp')), may hold values from 0 to 127
Outputs:
- slope: float32 [2, 128, 32768], P(None, None, ('blk', 'grp'))
Inputs may be any that keep to these rules, and one draw needn't show every extreme that they name: `neighbours`: places below 128 are the block's own emitters, the next 64 those listed by the previous block, the last 64 those listed by the next block. `send_list`: places in the listing block.
All inputs are finite; a program needn't handle non-finite values.
Results may differ from a plain program's by a relative error of at most 0.0012.
Values may be sent and summed in bfloat16 or wider, within the bound.
A program may use at most 64 MiB of HBM per device.

v0:
```python
import math
import jax
import jax.numpy as jnp
from jax import lax
from jax.sharding import PartitionSpec as P

section_weight = 0.25
phase_rate = 60.0
alpha_factor = 2.0


def from_behind(array, axis, by):
    size = lax.axis_size(axis)
    return lax.ppermute(array, axis, [(i, (i + by) % size) for i in range(size)])


def with_halo(cells, sides, width):
    for axis, dim in sides:
        count = lax.axis_size(axis)
        ends = count - 1
        head = lax.slice_in_dim(cells, 0, width, axis=dim)
        tail = lax.slice_in_dim(cells, cells.shape[dim] - width, cells.shape[dim], axis=dim)
        cells = jnp.concatenate(
            [
                lax.ppermute(tail, axis, [(i, (i + 1) % count) for i in range(ends)]),
                cells,
                lax.ppermute(head, axis, [((i + 1) % count, i) for i in range(ends)]),
            ],
            axis=dim,
        )
    return cells


def kernel_table(source_place, target_place, scaled):
    horizontal = target_place[0][None, :] - source_place[0][:, None]
    vertical = target_place[1][None, :] - source_place[1][:, None]
    phase = phase_rate * (horizontal * horizontal + vertical * vertical)
    cosine = (scaled * jnp.cos(phase)).astype(jnp.bfloat16)
    sine_part = (scaled * jnp.sin(phase)).astype(jnp.bfloat16)
    return jnp.concatenate([cosine, sine_part], axis=1)


def block_columns(total, fields, source_place, target_place, scaled):
    members = fields.shape[1]
    targets = target_place.shape[1]
    kernel = kernel_table(source_place, target_place, scaled)
    flat = fields.reshape(2 * members, fields.shape[2])
    product = jnp.dot(flat, kernel, preferred_element_type=jnp.float32)
    real_part = product[:members, :targets] - product[members:, targets:]
    imag_part = product[:members, targets:] + product[members:, :targets]
    return total + jnp.stack([real_part, imag_part])


def local(state, prev_slope, positions, pump, detuning, kappa, neighbours, send_list):
    members = state.shape[1]
    rows_here = state.shape[2]
    block_count = lax.axis_size("blk")
    group_size = lax.axis_size("grp")
    scaled = 1.0 / math.sqrt(rows_here * block_count * group_size)
    section_field = state + section_weight * prev_slope
    section_half = section_field.astype(jnp.bfloat16)
    my_index = lax.axis_index("blk")
    target_place = lax.all_gather(positions, "grp", axis=1, tiled=True)
    source_place = lax.all_gather(positions, "blk", axis=1, tiled=True)
    targets = target_place.shape[1]

    def place_of(block_index):
        return lax.dynamic_slice_in_dim(
            source_place, block_index % block_count * rows_here, rows_here, 1
        )

    def add_block(total, fields, block_index):
        return block_columns(total, fields, place_of(block_index), target_place, scaled)

    empty = jnp.zeros((2, members, targets), jnp.float32)

    def advance(step, carry):
        total, carried = carry
        carried = from_behind(carried, "blk", 1)
        return (add_block(total, carried, my_index - step), carried)

    total = add_block(empty, section_half, my_index)
    total, carried = lax.fori_loop(1, block_count, advance, (total, section_half))
    fresnel = lax.psum_scatter(total, "grp", scatter_dimension=2, tiled=True)
    halo_width = send_list.shape[1]
    to_prev = jnp.take(section_field, send_list[1], axis=2)
    to_next = jnp.take(section_field, send_list[0], axis=2)
    padded = with_halo(
        jnp.concatenate([to_prev, to_next], axis=2), ((("blk", "grp"), 2),), halo_width
    )
    local_buffer = jnp.concatenate(
        [section_field, padded[:, :, :halo_width], padded[:, :, 3 * halo_width :]], axis=2
    )
    coupled = jnp.zeros((2, members, rows_here), jnp.float32)
    for neighbour_slot in range(kappa.shape[0]):
        picked = jnp.take(local_buffer, neighbours[neighbour_slot], axis=2)
        coupled = coupled + kappa[neighbour_slot] * picked
    real_field = section_field[0]
    imag_field = section_field[1]
    modulus = real_field * real_field + imag_field * imag_field
    linear_real = pump - modulus
    linear_imag = detuning - alpha_factor * modulus
    local_real = linear_real * real_field - linear_imag * imag_field
    local_imag = linear_real * imag_field + linear_imag * real_field
    slope_real = local_real + fresnel[0] - coupled[1]
    slope_imag = local_imag + fresnel[1] + coupled[0]
    return jnp.stack([slope_real, slope_imag])


def solution(mesh):
    placed = (
        P(None, None, ("blk", "grp")),
        P(None, None, ("blk", "grp")),
        P(None, ("blk", "grp")),
        P(("blk", "grp")),
        P(("blk", "grp")),
        P(None, ("blk", "grp")),
        P(None, ("blk", "grp")),
        P(None, ("blk", "grp")),
    )
    return jax.shard_map(
        local, mesh=mesh, in_specs=placed, out_specs=P(None, None, ("blk", "grp")), check_vma=False
    )
```

profile of v0, /device:TPU:1, one launch (start us, length us, event | category | flops | bytes accessed | tf_op | source)
XLA Modules:
  0.0 357.1 jit_solution(1901654275807691150)
XLA Ops:
  6.5 30.5 %all_gather.7 = f32[2,2048]{1,0:T(2,128)S(1)} all-gather(f32[2,128]{1,0:T(2,128)} %param.16), channel_id=1, replica_groups=mesh['blk'=16,'grp'=16] {'blk'}, dimensions={1}, use_global_device_ids=true | all-gather | bytes 17408 | tf_op jit(solution)/shard_map/all_gather | solution.py:64
  37.1 31.7 %all_gather.6 = f32[2,2048]{1,0:T(2,128)S(1)} all-gather(f32[2,128]{1,0:T(2,128)} %param.16), channel_id=1, replica_groups=mesh['blk'=16,'grp'=16] {'grp'}, dimensions={1}, use_global_device_ids=true | all-gather | bytes 17408 | tf_op jit(solution)/shard_map/all_gather | solution.py:63
  68.8 1.0 fusion.18
  69.8 4.3 %multiply_convert_fusion.3 = (bf16[128,2048]{1,0:T(8,128)(2,1)S(1)}, bf16[128,2048]{1,0:T(8,128)(2,1)S(1)}) fusion(f32[128]{0:T(128)S(1)} %get-tuple-element.252, f32[2048]{0:T(1024)S(1)} %bitcast.118, f32[128]{0:T(128)S(1)} %get-tuple-element.251, f32[2048]{0:T(1024)S(1)} %bitcast.117), kind=kLoop, calls=%fused_computation.34 | loop fusion | flops 2621440 | bytes 1065984 | tf_op jit(solution)/shard_map/convert_element_type | solution.py:38
  75.1 1.5 pad_maximum_fusion
  76.6 1.9 copy.23
  78.5 102.8 %while.17 = (s32[]{:T(128)}, f32[2,128,2048]{1,2,0:T(8,128)S(1)}, bf16[2,128,128]{2,1,0:T(8,128)(2,1)S(1)}, f32[2,2048]{1,0:T(2,128)S(1)}, s32[]{:T(128)}, /*ind...) while((s32[]{:T(128)}, f32[2,128,2048]{1,2,0:T(8,128)S(1)}, ...), condition=%wide.region_1.2_spmd, body=%wide.region_0.1_spmd.sunk | while | flops 274726944 | bytes 19387720 | solution.py:83
  78.7 4.3 %multiply_convert_fusion.5 = (bf16[128,2048]{1,0:T(8,128)(2,1)S(1)}, bf16[128,2048]{1,0:T(8,128)(2,1)S(1)}) fusion(f32[128]{0:T(128)S(1)} %get-tuple-element.306, f32[2048]{0:T(1024)S(1)} %bitcast.115, f32[128]{0:T(128)S(1)} %get-tuple-element.308, f32[2048]{0:T(1024)S(1)} %bitcast.114), kind=kLoop, calls=%fused_computation.18.clone.1 | loop fusion | flops 2621440 | bytes 1065984 | tf_op jit(solution)/shard_map/while/body/eval_jaxpr/convert_element_type | solution.py:38
  83.0 1.2 collective-permute-done
  85.8 4.3 %multiply_convert_fusion.5 = (bf16[128,2048]{1,0:T(8,128)(2,1)S(1)}, bf16[128,2048]{1,0:T(8,128)(2,1)S(1)}) fusion(f32[128]{0:T(128)S(1)} %get-tuple-element.306, f32[2048]{0:T(1024)S(1)} %bitcast.115, f32[128]{0:T(128)S(1)} %get-tuple-element.308, f32[2048]{0:T(1024)S(1)} %bitcast.114), kind=kLoop, calls=%fused_computation.18.clone.1 | loop fusion | flops 2621440 | bytes 1065984 | tf_op jit(solution)/shard_map/while/body/eval_jaxpr/convert_element_type | solution.py:38
  92.6 4.3 %multiply_convert_fusion.5 = (bf16[128,2048]{1,0:T(8,128)(2,1)S(1)}, bf16[128,2048]{1,0:T(8,128)(2,1)S(1)}) fusion(f32[128]{0:T(128)S(1)} %get-tuple-element.306, f32[2048]{0:T(1024)S(1)} %bitcast.115, f32[128]{0:T(128)S(1)} %get-tuple-element.308, f32[2048]{0:T(1024)S(1)} %bitcast.114), kind=kLoop, calls=%fused_computation.18.clone.1 | loop fusion | flops 2621440 | bytes 1065984 | tf_op jit(solution)/shard_map/while/body/eval_jaxpr/convert_element_type | solution.py:38
  99.3 4.3 %multiply_convert_fusion.5 = (bf16[128,2048]{1,0:T(8,128)(2,1)S(1)}, bf16[128,2048]{1,0:T(8,128)(2,1)S(1)}) fusion(f32[128]{0:T(128)S(1)} %get-tuple-element.306, f32[2048]{0:T(1024)S(1)} %bitcast.115, f32[128]{0:T(128)S(1)} %get-tuple-element.308, f32[2048]{0:T(1024)S(1)} %bitcast.114), kind=kLoop, calls=%fused_computation.18.clone.1 | loop fusion | flops 2621440 | bytes 1065984 | tf_op jit(solution)/shard_map/while/body/eval_jaxpr/convert_element_type | solution.py:38
  106.0 4.3 %multiply_convert_fusion.5 = (bf16[128,2048]{1,0:T(8,128)(2,1)S(1)}, bf16[128,2048]{1,0:T(8,128)(2,1)S(1)}) fusion(f32[128]{0:T(128)S(1)} %get-tuple-element.306, f32[2048]{0:T(1024)S(1)} %bitcast.115, f32[128]{0:T(128)S(1)} %get-tuple-element.308, f32[2048]{0:T(1024)S(1)} %bitcast.114), kind=kLoop, calls=%fused_computation.18.clone.1 | loop fusion | flops 2621440 | bytes 1065984 | tf_op jit(solution)/shard_map/while/body/eval_jaxpr/convert_element_type | solution.py:38
  112.8 4.3 %multiply_convert_fusion.5 = (bf16[128,2048]{1,0:T(8,128)(2,1)S(1)}, bf16[128,2048]{1,0:T(8,128)(2,1)S(1)}) fusion(f32[128]{0:T(128)S(1)} %get-tuple-element.306, f32[2048]{0:T(1024)S(1)} %bitcast.115, f32[128]{0:T(128)S(1)} %get-tuple-element.308, f32[2048]{0:T(1024)S(1)} %bitcast.114), kind=kLoop, calls=%fused_computation.18.clone.1 | loop fusion | flops 2621440 | bytes 1065984 | tf_op jit(solution)/shard_map/while/body/eval_jaxpr/convert_element_type | solution.py:38
  119.5 4.3 %multiply_convert_fusion.5 = (bf16[128,2048]{1,0:T(8,128)(2,1)S(1)}, bf16[128,2048]{1,0:T(8,128)(2,1)S(1)}) fusion(f32[128]{0:T(128)S(1)} %get-tuple-element.306, f32[2048]{0:T(1024)S(1)} %bitcast.115, f32[128]{0:T(128)S(1)} %get-tuple-element.308, f32[2048]{0:T(1024)S(1)} %bitcast.114), kind=kLoop, calls=%fused_computation.18.clone.1 | loop fusion | flops 2621440 | bytes 1065984 | tf_op jit(solution)/shard_map/while/body/eval_jaxpr/convert_element_type | solution.py:38
  123.8 0.9 collective-permute-done
  126.7 4.3 %multiply_convert_fusion.5 = (bf16[128,2048]{1,0:T(8,128)(2,1)S(1)}, bf16[128,2048]{1,0:T(8,128)(2,1)S(1)}) fusion(f32[128]{0:T(128)S(1)} %get-tuple-element.306, f32[2048]{0:T(1024)S(1)} %bitcast.115, f32[128]{0:T(128)S(1)} %get-tuple-element.308, f32[2048]{0:T(1024)S(1)} %bitcast.114), kind=kLoop, calls=%fused_computation.18.clone.1 | loop fusion | flops 2621440 | bytes 1065984 | tf_op jit(solution)/shard_map/while/body/eval_jaxpr/convert_element_type | solution.py:38
  131.0 1.0 collective-permute-done
  133.9 4.3 %multiply_convert_fusion.5 = (bf16[128,2048]{1,0:T(8,128)(2,1)S(1)}, bf16[128,2048]{1,0:T(8,128)(2,1)S(1)}) fusion(f32[128]{0:T(128)S(1)} %get-tuple-element.306, f32[2048]{0:T(1024)S(1)} %bitcast.115, f32[128]{0:T(128)S(1)} %get-tuple-element.308, f32[2048]{0:T(1024)S(1)} %bitcast.114), kind=kLoop, calls=%fused_computation.18.clone.1 | loop fusion | flops 2621440 | bytes 1065984 | tf_op jit(solution)/shard_map/while/body/eval_jaxpr/convert_element_type | solution.py:38
  140.6 4.3 %multiply_convert_fusion.5 = (bf16[128,2048]{1,0:T(8,128)(2,1)S(1)}, bf16[128,2048]{1,0:T(8,128)(2,1)S(1)}) fusion(f32[128]{0:T(128)S(1)} %get-tuple-element.306, f32[2048]{0:T(1024)S(1)} %bitcast.115, f32[128]{0:T(128)S(1)} %get-tuple-element.308, f32[2048]{0:T(1024)S(1)} %bitcast.114), kind=kLoop, calls=%fused_computation.18.clone.1 | loop fusion | flops 2621440 | bytes 1065984 | tf_op jit(solution)/shard_map/while/body/eval_jaxpr/convert_element_type | solution.py:38
  147.4 4.3 %multiply_convert_fusion.5 = (bf16[128,2048]{1,0:T(8,128)(2,1)S(1)}, bf16[128,2048]{1,0:T(8,128)(2,1)S(1)}) fusion(f32[128]{0:T(128)S(1)} %get-tuple-element.306, f32[2048]{0:T(1024)S(1)} %bitcast.115, f32[128]{0:T(128)S(1)} %get-tuple-element.308, f32[2048]{0:T(1024)S(1)} %bitcast.114), kind=kLoop, calls=%fused_computation.18.clone.1 | loop fusion | flops 2621440 | bytes 1065984 | tf_op jit(solution)/shard_map/while/body/eval_jaxpr/convert_element_type | solution.py:38
  154.1 4.3 %multiply_convert_fusion.5 = (bf16[128,2048]{1,0:T(8,128)(2,1)S(1)}, bf16[128,2048]{1,0:T(8,128)(2,1)S(1)}) fusion(f32[128]{0:T(128)S(1)} %get-tuple-element.306, f32[2048]{0:T(1024)S(1)} %bitcast.115, f32[128]{0:T(128)S(1)} %get-tuple-element.308, f32[2048]{0:T(1024)S(1)} %bitcast.114), kind=kLoop, calls=%fused_computation.18.clone.1 | loop fusion | flops 2621440 | bytes 1065984 | tf_op jit(solution)/shard_map/while/body/eval_jaxpr/convert_element_type | solution.py:38
  160.9 4.3 %multiply_convert_fusion.5 = (bf16[128,2048]{1,0:T(8,128)(2,1)S(1)}, bf16[128,2048]{1,0:T(8,128)(2,1)S(1)}) fusion(f32[128]{0:T(128)S(1)} %get-tuple-element.306, f32[2048]{0:T(1024)S(1)} %bitcast.115, f32[128]{0:T(128)S(1)} %get-tuple-element.308, f32[2048]{0:T(1024)S(1)} %bitcast.114), kind=kLoop, calls=%fused_computation.18.clone.1 | loop fusion | flops 2621440 | bytes 1065984 | tf_op jit(solution)/shard_map/while/body/eval_jaxpr/convert_element_type | solution.py:38
  167.6 4.3 %multiply_convert_fusion.5 = (bf16[128,2048]{1,0:T(8,128)(2,1)S(1)}, bf16[128,2048]{1,0:T(8,128)(2,1)S(1)}) fusion(f32[128]{0:T(128)S(1)} %get-tuple-element.306, f32[2048]{0:T(1024)S(1)} %bitcast.115, f32[128]{0:T(128)S(1)} %get-tuple-element.308, f32[2048]{0:T(1024)S(1)} %bitcast.114), kind=kLoop, calls=%fused_computation.18.clone.1 | loop fusion | flops 2621440 | bytes 1065984 | tf_op jit(solution)/shard_map/while/body/eval_jaxpr/convert_element_type | solution.py:38
  174.4 4.3 %multiply_convert_fusion.5 = (bf16[128,2048]{1,0:T(8,128)(2,1)S(1)}, bf16[128,2048]{1,0:T(8,128)(2,1)S(1)}) fusion(f32[128]{0:T(128)S(1)} %get-tuple-element.306, f32[2048]{0:T(1024)S(1)} %bitcast.115, f32[128]{0:T(128)S(1)} %get-tuple-element.308, f32[2048]{0:T(1024)S(1)} %bitcast.114), kind=kLoop, calls=%fused_computation.18.clone.1 | loop fusion | flops 2621440 | bytes 1065984 | tf_op jit(solution)/shard_map/while/body/eval_jaxpr/convert_element_type | solution.py:38
  178.7 1.2 collective-permute-done
  181.3 8.5 %copy.24 = f32[2,128,2048]{1,0,2:T(2,128)} copy(f32[2,128,2048]{1,2,0:T(8,128)S(1)} %get-tuple-element.162) | data formatting | bytes 4194304 | tf_op jit(solution)/shard_map/while | solution.py:83
  191.3 16.5 %collective-permute-start.1 = (f32[2,128,64]{2,1,0:T(8,128)S(1)}, f32[2,128,64]{2,1,0:T(8,128)S(1)}, u32[]{:S(2)}, u32[]{:S(2)}) collective-permute-start(f32[2,128,64]{2,1,0:T(8,128)S(1)} %select_bitcast_fusion.1), channel_id=1, source_target_pairs={{0,1},{1,2},{2,3},{3,4},{4,5},{5,6},{6,7},{7,8},{8,9},{9,10},{10,1... | collective-permute-start | bytes 196616 | tf_op jit(solution)/shard_map/ppermute | solution.py:25
  208.7 3.2 collective-permute-start.2
  213.2 5.7 %collective-permute-done.2 = f32[2,128,64]{2,1,0:T(8,128)S(1)} collective-permute-done((f32[2,128,64]{2,1,0:T(8,128)S(1)}, f32[2,128,64]{2,1,0:T(8,128)S(1)}, u32[]{:S(2)}, u32[]{:S(2)}) %collective-permute-start.2) | collective-permute-done | bytes 65568 | tf_op jit(solution)/shard_map/ppermute | solution.py:27
  224.4 123.8 %all-reduce.3.cloned.1.call-done = f32[2,128,2048]{1,0,2:T(2,128)} async-done(((f32[2,128,2048]{1,0,2:T(2,128)}), f32[2,128,2048]{1,0,2:T(2,128)}) %all-reduce.3.cloned.1.call-update) | async-done | bytes 2097168
  348.2 1.1 constant_dynamic-slice_fusion.1
  (186 shorter events, 43.4 us)
Async XLA Ops:
  6.5 341.7 %all-reduce.3.cloned.1.call-start = ((), (), s32[]{:S(2)}) async-start(), calls=%async_computation | async-start | bytes 4194304
  78.5 5.7 %collective-permute-start = (bf16[2,128,128]{2,1,0:T(8,128)(2,1)S(1)}, bf16[2,128,128]{2,1,0:T(8,128)(2,1)S(1)}, u32[]{:S(2)}, u32[]{:S(2)}) collective-permute-start(bf16[2,128,128]{2,1,0:T(8,128)(2,1)S(1)} %get-tuple-element.328), channel_id=1, source_target_pairs={{0,16},{16,32},{32,48},{48,64},{64,80},{80,96},{96,112},{112,128},... | collective-permute-start | bytes 196616 | tf_op jit(solution)/shard_map/while/body/eval_jaxpr/ppermute | solution.py:14
  85.6 5.3 %collective-permute-start = (bf16[2,128,128]{2,1,0:T(8,128)(2,1)S(1)}, bf16[2,128,128]{2,1,0:T(8,128)(2,1)S(1)}, u32[]{:S(2)}, u32[]{:S(2)}) collective-permute-start(bf16[2,128,128]{2,1,0:T(8,128)(2,1)S(1)} %get-tuple-element.328), channel_id=1, source_target_pairs={{0,16},{16,32},{32,48},{48,64},{64,80},{80,96},{96,112},{112,128},... | collective-permute-start | bytes 196616 | tf_op jit(solution)/shard_map/while/body/eval_jaxpr/ppermute | solution.py:14
  92.4 5.3 %collective-permute-start = (bf16[2,128,128]{2,1,0:T(8,128)(2,1)S(1)}, bf16[2,128,128]{2,1,0:T(8,128)(2,1)S(1)}, u32[]{:S(2)}, u32[]{:S(2)}) collective-permute-start(bf16[2,128,128]{2,1,0:T(8,128)(2,1)S(1)} %get-tuple-element.328), channel_id=1, source_target_pairs={{0,16},{16,32},{32,48},{48,64},{64,80},{80,96},{96,112},{112,128},... | collective-permute-start | bytes 196616 | tf_op jit(solution)/shard_map/while/body/eval_jaxpr/ppermute | solution.py:14
  99.1 5.3 %collective-permute-start = (bf16[2,128,128]{2,1,0:T(8,128)(2,1)S(1)}, bf16[2,128,128]{2,1,0:T(8,128)(2,1)S(1)}, u32[]{:S(2)}, u32[]{:S(2)}) collective-permute-start(bf16[2,128,128]{2,1,0:T(8,128)(2,1)S(1)} %get-tuple-element.328), channel_id=1, source_target_pairs={{0,16},{16,32},{32,48},{48,64},{64,80},{80,96},{96,112},{112,128},... | collective-permute-start | bytes 196616 | tf_op jit(solution)/shard_map/while/body/eval_jaxpr/ppermute | solution.py:14
  105.9 5.3 %collective-permute-start = (bf16[2,128,128]{2,1,0:T(8,128)(2,1)S(1)}, bf16[2,128,128]{2,1,0:T(8,128)(2,1)S(1)}, u32[]{:S(2)}, u32[]{:S(2)}) collective-permute-start(bf16[2,128,128]{2,1,0:T(8,128)(2,1)S(1)} %get-tuple-element.328), channel_id=1, source_target_pairs={{0,16},{16,32},{32,48},{48,64},{64,80},{80,96},{96,112},{112,128},... | collective-permute-start | bytes 196616 | tf_op jit(solution)/shard_map/while/body/eval_jaxpr/ppermute | solution.py:14
  112.6 5.3 %collective-permute-start = (bf16[2,128,128]{2,1,0:T(8,128)(2,1)S(1)}, bf16[2,128,128]{2,1,0:T(8,128)(2,1)S(1)}, u32[]{:S(2)}, u32[]{:S(2)}) collective-permute-start(bf16[2,128,128]{2,1,0:T(8,128)(2,1)S(1)} %get-tuple-element.328), channel_id=1, source_target_pairs={{0,16},{16,32},{32,48},{48,64},{64,80},{80,96},{96,112},{112,128},... | collective-permute-start | bytes 196616 | tf_op jit(solution)/shard_map/while/body/eval_jaxpr/ppermute | solution.py:14
  119.4 5.3 %collective-permute-start = (bf16[2,128,128]{2,1,0:T(8,128)(2,1)S(1)}, bf16[2,128,128]{2,1,0:T(8,128)(2,1)S(1)}, u32[]{:S(2)}, u32[]{:S(2)}) collective-permute-start(bf16[2,128,128]{2,1,0:T(8,128)(2,1)S(1)} %get-tuple-element.328), channel_id=1, source_target_pairs={{0,16},{16,32},{32,48},{48,64},{64,80},{80,96},{96,112},{112,128},... | collective-permute-start | bytes 196616 | tf_op jit(solution)/shard_map/while/body/eval_jaxpr/ppermute | solution.py:14
  126.1 5.8 %collective-permute-start = (bf16[2,128,128]{2,1,0:T(8,128)(2,1)S(1)}, bf16[2,128,128]{2,1,0:T(8,128)(2,1)S(1)}, u32[]{:S(2)}, u32[]{:S(2)}) collective-permute-start(bf16[2,128,128]{2,1,0:T(8,128)(2,1)S(1)} %get-tuple-element.328), channel_id=1, source_target_pairs={{0,16},{16,32},{32,48},{48,64},{64,80},{80,96},{96,112},{112,128},... | collective-permute-start | bytes 196616 | tf_op jit(solution)/shard_map/while/body/eval_jaxpr/ppermute | solution.py:14
  133.4 5.3 %collective-permute-start = (bf16[2,128,128]{2,1,0:T(8,128)(2,1)S(1)}, bf16[2,128,128]{2,1,0:T(8,128)(2,1)S(1)}, u32[]{:S(2)}, u32[]{:S(2)}) collective-permute-start(bf16[2,128,128]{2,1,0:T(8,128)(2,1)S(1)} %get-tuple-element.328), channel_id=1, source_target_pairs={{0,16},{16,32},{32,48},{48,64},{64,80},{80,96},{96,112},{112,128},... | collective-permute-start | bytes 196616 | tf_op jit(solution)/shard_map/while/body/eval_jaxpr/ppermute | solution.py:14
  140.2 5.3 %collective-permute-start = (bf16[2,128,128]{2,1,0:T(8,128)(2,1)S(1)}, bf16[2,128,128]{2,1,0:T(8,128)(2,1)S(1)}, u32[]{:S(2)}, u32[]{:S(2)}) collective-permute-start(bf16[2,128,128]{2,1,0:T(8,128)(2,1)S(1)} %get-tuple-element.328), channel_id=1, source_target_pairs={{0,16},{16,32},{32,48},{48,64},{64,80},{80,96},{96,112},{112,128},... | collective-permute-start | bytes 196616 | tf_op jit(solution)/shard_map/while/body/eval_jaxpr/ppermute | solution.py:14
  146.9 5.3 %collective-permute-start = (bf16[2,128,128]{2,1,0:T(8,128)(2,1)S(1)}, bf16[2,128,128]{2,1,0:T(8,128)(2,1)S(1)}, u32[]{:S(2)}, u32[]{:S(2)}) collective-permute-start(bf16[2,128,128]{2,1,0:T(8,128)(2,1)S(1)} %get-tuple-element.328), channel_id=1, source_target_pairs={{0,16},{16,32},{32,48},{48,64},{64,80},{80,96},{96,112},{112,128},... | collective-permute-start | bytes 196616 | tf_op jit(solution)/shard_map/while/body/eval_jaxpr/ppermute | solution.py:14
  153.7 5.3 %collective-permute-start = (bf16[2,128,128]{2,1,0:T(8,128)(2,1)S(1)}, bf16[2,128,128]{2,1,0:T(8,128)(2,1)S(1)}, u32[]{:S(2)}, u32[]{:S(2)}) collective-permute-start(bf16[2,128,128]{2,1,0:T(8,128)(2,1)S(1)} %get-tuple-element.328), channel_id=1, source_target_pairs={{0,16},{16,32},{32,48},{48,64},{64,80},{80,96},{96,112},{112,128},... | collective-permute-start | bytes 196616 | tf_op jit(solution)/shard_map/while/body/eval_jaxpr/ppermute | solution.py:14
  160.4 5.3 %collective-permute-start = (bf16[2,128,128]{2,1,0:T(8,128)(2,1)S(1)}, bf16[2,128,128]{2,1,0:T(8,128)(2,1)S(1)}, u32[]{:S(2)}, u32[]{:S(2)}) collective-permute-start(bf16[2,128,128]{2,1,0:T(8,128)(2,1)S(1)} %get-tuple-element.328), channel_id=1, source_target_pairs={{0,16},{16,32},{32,48},{48,64},{64,80},{80,96},{96,112},{112,128},... | collective-permute-start | bytes 196616 | tf_op jit(solution)/shard_map/while/body/eval_jaxpr/ppermute | solution.py:14
  167.1 5.3 %collective-permute-start = (bf16[2,128,128]{2,1,0:T(8,128)(2,1)S(1)}, bf16[2,128,128]{2,1,0:T(8,128)(2,1)S(1)}, u32[]{:S(2)}, u32[]{:S(2)}) collective-permute-start(bf16[2,128,128]{2,1,0:T(8,128)(2,1)S(1)} %get-tuple-element.328), channel_id=1, source_target_pairs={{0,16},{16,32},{32,48},{48,64},{64,80},{80,96},{96,112},{112,128},... | collective-permute-start | bytes 196616 | tf_op jit(solution)/shard_map/while/body/eval_jaxpr/ppermute | solution.py:14
  173.9 6.0 %collective-permute-start = (bf16[2,128,128]{2,1,0:T(8,128)(2,1)S(1)}, bf16[2,128,128]{2,1,0:T(8,128)(2,1)S(1)}, u32[]{:S(2)}, u32[]{:S(2)}) collective-permute-start(bf16[2,128,128]{2,1,0:T(8,128)(2,1)S(1)} %get-tuple-element.328), channel_id=1, source_target_pairs={{0,16},{16,32},{32,48},{48,64},{64,80},{80,96},{96,112},{112,128},... | collective-permute-start | bytes 196616 | tf_op jit(solution)/shard_map/while/body/eval_jaxpr/ppermute | solution.py:14
  189.9 0.7 copy-start.2
  189.9 22.0 %copy-start.5 = (u32[256]{0:T(256)S(1)}, u32[256]{0:T(256)}, u32[]{:S(2)}) copy-start(u32[256]{0:T(256)} %constant.141) | copy-start | bytes 3076
  189.9 23.3 %copy-start.1 = (s32[6,128]{1,0:T(8,128)S(1)}, s32[6,128]{1,0:T(8,128)}, u32[]{:S(2)}) copy-start(s32[6,128]{1,0:T(8,128)} %param.20) | copy-start | bytes 9220
  189.9 23.3 %copy-start = (f32[6,128]{1,0:T(8,128)S(1)}, f32[6,128]{1,0:T(8,128)}, u32[]{:S(2)}) copy-start(f32[6,128]{1,0:T(8,128)} %param.19) | copy-start | bytes 9220
  191.3 21.9 %collective-permute-start.1 = (f32[2,128,64]{2,1,0:T(8,128)S(1)}, f32[2,128,64]{2,1,0:T(8,128)S(1)}, u32[]{:S(2)}, u32[]{:S(2)}) collective-permute-start(f32[2,128,64]{2,1,0:T(8,128)S(1)} %select_bitcast_fusion.1), channel_id=1, source_target_pairs={{0,1},{1,2},{2,3},{3,4},{4,5},{5,6},{6,7},{7,8},{8,9},{9,10},{10,1... | collective-permute-start | bytes 196616 | tf_op jit(solution)/shard_map/ppermute | solution.py:25
  208.7 10.2 %collective-permute-start.2 = (f32[2,128,64]{2,1,0:T(8,128)S(1)}, f32[2,128,64]{2,1,0:T(8,128)S(1)}, u32[]{:S(2)}, u32[]{:S(2)}) collective-permute-start(f32[2,128,64]{2,1,0:T(8,128)S(1)} %select_bitcast_fusion), channel_id=1, source_target_pairs={{1,0},{2,1},{3,2},{4,3},{5,4},{6,5},{7,6},{8,7},{9,8},{10,9},{11,1... | collective-permute-start | bytes 196616 | tf_op jit(solution)/shard_map/ppermute | solution.py:27
  220.0 129.5 %copy-start.3 = (f32[128]{0:T(128)S(1)}, f32[128]{0:T(128)}, u32[]{:S(2)}) copy-start(f32[128]{0:T(128)} %param.18) | copy-start | bytes 1540
  220.0 129.5 %copy-start.4 = (f32[128]{0:T(128)S(1)}, f32[128]{0:T(128)}, u32[]{:S(2)}) copy-start(f32[128]{0:T(128)} %param.17) | copy-start | bytes 1540
Sparse Core Ops, SparseCore 0:
  190.0 158.1 all-reduce.2
where the time goes:
time: 357 us
  waiting for transfers between devices  141 us (39%)
  other arithmetic  82.2 us (23%)
  blocking collectives  62.2 us (17%)
  starting transfers between devices  23.9 us (7%)
  local copies, waits for them, and re-layouts  20.2 us (6%)
  between operations  14.4 us (4%)
  matrix products  11.8 us (3%)
    unnamed x2, waiting for transfers between devices  124 us
    convert_element_type x16, other arithmetic, kernel_table(): cosine = (scaled * jnp.cos(phase)).astype(jnp.bfloat16)  68.5 us
    all_gather x1, blocking collectives, local(): target_place = lax.all_gather(positions, 'grp', axis=1, tiled=True)  31.7 us
    all_gather x1, blocking collectives, local(): source_place = lax.all_gather(positions, 'blk', axis=1, tiled=True)  30.5 us
    ppermute x1, starting transfers between devices, with_halo(): lax.ppermute(tail, axis, [(i, (i + 1) % count) for i in range(ends)])  16.5 us
    ppermute x15, waiting for transfers between devices, from_behind(): lax.ppermute(array, axis, [(i, (i + by) % size) for i in range(size)])  11.9 us
    dot_general x16, matrix products, block_columns(): product = jnp.dot(flat, kernel, preferred_element_type=jnp.float32)  11.8 us
    while x2, local copies, waits for them, and re-layouts, local(): lax.fori_loop(1, block_count, advance, (total, section_half))  10.4 us
  transfers between devices with their start and end apart: 18, of which 17 were waited for; matrix products, arithmetic and copies ran while one was open for 20% of the time, Pallas kernels for 0%

commit v1 on v0

--- a/solution.py
+++ b/solution.py
@@ -61,7 +61,8 @@
     section_half = section_field.astype(jnp.bfloat16)
     my_index = lax.axis_index("blk")
     target_place = lax.all_gather(positions, "grp", axis=1, tiled=True)
-    source_place = lax.all_gather(positions, "blk", axis=1, tiled=True)
+    sent = jnp.stack([positions] * lax.axis_size("blk"))
+    source_place = jnp.concatenate(lax.all_to_all(sent, "blk", 0, 0), axis=1)
     targets = target_place.shape[1]
 
     def place_of(block_index):

time: 357 us -> 336 us (0.941)
  blocking collectives: 62.2 us -> 25 us
  starting transfers between devices: 23.9 us -> 40.4 us
    all_gather x1 -> x0, blocking collectives: 30.5 us -> none  [local(): source_place = lax.all_gather(positions, 'blk', axis=1, tiled=True)]
    all_to_all x0 -> x1, starting transfers between devices: none -> 10.1 us  [local(): source_place = jnp.concatenate(lax.all_to_all(sent, 'blk', 0, 0), axis=1)]
    ppermute x15, starting transfers between devices: 4.14 us -> 14.1 us  [from_behind(): lax.ppermute(array, axis, [(i, (i + by) % size) for i in range(size)])]
    all_gather x1, blocking collectives: 31.7 us -> 25 us  [local(): target_place = lax.all_gather(positions, 'grp', axis=1, tiled=True)]
    ppermute x15, waiting for transfers between devices: 11.9 us -> 5.66 us  [from_behind(): lax.ppermute(array, axis, [(i, (i + by) % size) for i in range(size)])]
    unnamed x2, waiting for transfers between devices: 124 us -> 130 us
  transfers between devices with their start and end apart: 18 -> 19, of which waited for: 17 -> 11; matrix products, arithmetic and copies ran while one was open for 20% -> 22% of each run, Pallas kernels for 0% -> 0%
where the time goes in v1:
time: 336 us
  waiting for transfers between devices  139 us (41%)
  other arithmetic  82.2 us (24%)
  starting transfers between devices  40.4 us (12%)
  blocking collectives  25 us (7%)
  local copies, waits for them, and re-layouts  21.5 us (6%)
  between operations  14.4 us (4%)
  matrix products  11.8 us (4%)
    unnamed x2, waiting for transfers between devices  130 us
    convert_element_type x16, other arithmetic, kernel_table(): cosine = (scaled * jnp.cos(phase)).astype(jnp.bfloat16)  68.5 us
    all_gather x1, blocking collectives, local(): target_place = lax.all_gather(positions, 'grp', axis=1, tiled=True)  25 us
    ppermute x15, starting transfers between devices, from_behind(): lax.ppermute(array, axis, [(i, (i + by) % size) for i in range(size)])  14.1 us
    ppermute x1, starting transfers between devices, with_halo(): lax.ppermute(tail, axis, [(i, (i + 1) % count) for i in range(ends)])  13.4 us
    dot_general x16, matrix products, block_columns(): product = jnp.dot(flat, kernel, preferred_element_type=jnp.float32)  11.8 us
    while x2, local copies, waits for them, and re-layouts, local(): lax.fori_loop(1, block_count, advance, (total, section_half))  10.4 us
    all_to_all x1, starting transfers between devices, local(): source_place = jnp.concatenate(lax.all_to_all(sent, 'blk', 0, 0), axis=1)  10.1 us
  transfers between devices with their start and end apart: 19, of which 11 were waited for; matrix products, arithmetic and copies ran while one was open for 22% of the time, Pallas kernels for 0%

profile of v1, /device:TPU:1, one launch (start us, length us, event | category | flops | bytes accessed | tf_op | source)
XLA Modules:
  0.0 335.5 jit_solution(1115007951686455971)
XLA Ops:
  6.5 1.3 stack.63
  7.8 10.1 %all-to-all-start = ((f32[16,2,128]{2,1,0:T(2,128)}), f32[16,2,128]{2,1,0:T(2,128)S(1)}, u32[]{:S(2)}, u32[]{:S(2)}) async-start(f32[16,2,128]{2,1,0:T(2,128)} %stack.63), calls=%async_computation | async-start | bytes 32768 | tf_op jit(solution)/shard_map/all_to_all | solution.py:65
  18.0 25.0 %all_gather.3 = f32[2,2048]{1,0:T(2,128)S(1)} all-gather(f32[2,128]{1,0:T(2,128)} %param.16), channel_id=1, replica_groups=mesh['blk'=16,'grp'=16] {'grp'}, dimensions={1}, use_global_device_ids=true | all-gather | bytes 17408 | tf_op jit(solution)/shard_map/all_gather | solution.py:63
  44.1 4.3 %multiply_convert_fusion.3 = (bf16[128,2048]{1,0:T(8,128)(2,1)S(1)}, bf16[128,2048]{1,0:T(8,128)(2,1)S(1)}) fusion(f32[128]{0:T(128)S(1)} %get-tuple-element.252, f32[2048]{0:T(1024)S(1)} %bitcast.121, f32[128]{0:T(128)S(1)} %get-tuple-element.251, f32[2048]{0:T(1024)S(1)} %bitcast.120), kind=kLoop, calls=%fused_computation.34 | loop fusion | flops 2621440 | bytes 1065984 | tf_op jit(solution)/shard_map/convert_element_type | solution.py:38
  49.4 1.6 pad_maximum_fusion
  50.9 1.9 copy.23
  52.9 106.5 %while.17 = (s32[]{:T(128)}, f32[2,128,2048]{1,2,0:T(8,128)S(1)}, bf16[2,128,128]{2,1,0:T(8,128)(2,1)S(1)}, f32[2,2048]{1,0:T(2,128)S(1)}, s32[]{:T(128)}, /*ind...) while((s32[]{:T(128)}, f32[2,128,2048]{1,2,0:T(8,128)S(1)}, ...), condition=%wide.region_1.2_spmd, body=%wide.region_0.1_spmd.sunk | while | flops 274726944 | bytes 19387720 | solution.py:84
  54.0 4.3 %multiply_convert_fusion.5 = (bf16[128,2048]{1,0:T(8,128)(2,1)S(1)}, bf16[128,2048]{1,0:T(8,128)(2,1)S(1)}) fusion(f32[128]{0:T(128)S(1)} %get-tuple-element.306, f32[2048]{0:T(1024)S(1)} %bitcast.118, f32[128]{0:T(128)S(1)} %get-tuple-element.308, f32[2048]{0:T(1024)S(1)} %bitcast.117), kind=kLoop, calls=%fused_computation.18.clone.1 | loop fusion | flops 2621440 | bytes 1065984 | tf_op jit(solution)/shard_map/while/body/eval_jaxpr/convert_element_type | solution.py:38
  60.0 1.6 collective-permute-start
  61.6 4.3 %multiply_convert_fusion.5 = (bf16[128,2048]{1,0:T(8,128)(2,1)S(1)}, bf16[128,2048]{1,0:T(8,128)(2,1)S(1)}) fusion(f32[128]{0:T(128)S(1)} %get-tuple-element.306, f32[2048]{0:T(1024)S(1)} %bitcast.118, f32[128]{0:T(128)S(1)} %get-tuple-element.308, f32[2048]{0:T(1024)S(1)} %bitcast.117), kind=kLoop, calls=%fused_computation.18.clone.1 | loop fusion | flops 2621440 | bytes 1065984 | tf_op jit(solution)/shard_map/while/body/eval_jaxpr/convert_element_type | solution.py:38
  68.1 4.3 %multiply_convert_fusion.5 = (bf16[128,2048]{1,0:T(8,128)(2,1)S(1)}, bf16[128,2048]{1,0:T(8,128)(2,1)S(1)}) fusion(f32[128]{0:T(128)S(1)} %get-tuple-element.306, f32[2048]{0:T(1024)S(1)} %bitcast.118, f32[128]{0:T(128)S(1)} %get-tuple-element.308, f32[2048]{0:T(1024)S(1)} %bitcast.117), kind=kLoop, calls=%fused_computation.18.clone.1 | loop fusion | flops 2621440 | bytes 1065984 | tf_op jit(solution)/shard_map/while/body/eval_jaxpr/convert_element_type | solution.py:38
  74.1 1.6 collective-permute-start
  75.7 4.3 %multiply_convert_fusion.5 = (bf16[128,2048]{1,0:T(8,128)(2,1)S(1)}, bf16[128,2048]{1,0:T(8,128)(2,1)S(1)}) fusion(f32[128]{0:T(128)S(1)} %get-tuple-element.306, f32[2048]{0:T(1024)S(1)} %bitcast.118, f32[128]{0:T(128)S(1)} %get-tuple-element.308, f32[2048]{0:T(1024)S(1)} %bitcast.117), kind=kLoop, calls=%fused_computation.18.clone.1 | loop fusion | flops 2621440 | bytes 1065984 | tf_op jit(solution)/shard_map/while/body/eval_jaxpr/convert_element_type | solution.py:38
  82.1 4.3 %multiply_convert_fusion.5 = (bf16[128,2048]{1,0:T(8,128)(2,1)S(1)}, bf16[128,2048]{1,0:T(8,128)(2,1)S(1)}) fusion(f32[128]{0:T(128)S(1)} %get-tuple-element.306, f32[2048]{0:T(1024)S(1)} %bitcast.118, f32[128]{0:T(128)S(1)} %get-tuple-element.308, f32[2048]{0:T(1024)S(1)} %bitcast.117), kind=kLoop, calls=%fused_computation.18.clone.1 | loop fusion | flops 2621440 | bytes 1065984 | tf_op jit(solution)/shard_map/while/body/eval_jaxpr/convert_element_type | solution.py:38
  88.2 1.5 collective-permute-start
  89.8 4.3 %multiply_convert_fusion.5 = (bf16[128,2048]{1,0:T(8,128)(2,1)S(1)}, bf16[128,2048]{1,0:T(8,128)(2,1)S(1)}) fusion(f32[128]{0:T(128)S(1)} %get-tuple-element.306, f32[2048]{0:T(1024)S(1)} %bitcast.118, f32[128]{0:T(128)S(1)} %get-tuple-element.308, f32[2048]{0:T(1024)S(1)} %bitcast.117), kind=kLoop, calls=%fused_computation.18.clone.1 | loop fusion | flops 2621440 | bytes 1065984 | tf_op jit(solution)/shard_map/while/body/eval_jaxpr/convert_element_type | solution.py:38
  96.2 4.3 %multiply_convert_fusion.5 = (bf16[128,2048]{1,0:T(8,128)(2,1)S(1)}, bf16[128,2048]{1,0:T(8,128)(2,1)S(1)}) fusion(f32[128]{0:T(128)S(1)} %get-tuple-element.306, f32[2048]{0:T(1024)S(1)} %bitcast.118, f32[128]{0:T(128)S(1)} %get-tuple-element.308, f32[2048]{0:T(1024)S(1)} %bitcast.117), kind=kLoop, calls=%fused_computation.18.clone.1 | loop fusion | flops 2621440 | bytes 1065984 | tf_op jit(solution)/shard_map/while/body/eval_jaxpr/convert_element_type | solution.py:38
  102.3 2.7 collective-permute-start
  105.0 4.3 %multiply_convert_fusion.5 = (bf16[128,2048]{1,0:T(8,128)(2,1)S(1)}, bf16[128,2048]{1,0:T(8,128)(2,1)S(1)}) fusion(f32[128]{0:T(128)S(1)} %get-tuple-element.306, f32[2048]{0:T(1024)S(1)} %bitcast.118, f32[128]{0:T(128)S(1)} %get-tuple-element.308, f32[2048]{0:T(1024)S(1)} %bitcast.117), kind=kLoop, calls=%fused_computation.18.clone.1 | loop fusion | flops 2621440 | bytes 1065984 | tf_op jit(solution)/shard_map/while/body/eval_jaxpr/convert_element_type | solution.py:38
  110.8 1.4 collective-permute-start
  112.2 4.3 %multiply_convert_fusion.5 = (bf16[128,2048]{1,0:T(8,128)(2,1)S(1)}, bf16[128,2048]{1,0:T(8,128)(2,1)S(1)}) fusion(f32[128]{0:T(128)S(1)} %get-tuple-element.306, f32[2048]{0:T(1024)S(1)} %bitcast.118, f32[128]{0:T(128)S(1)} %get-tuple-element.308, f32[2048]{0:T(1024)S(1)} %bitcast.117), kind=kLoop, calls=%fused_computation.18.clone.1 | loop fusion | flops 2621440 | bytes 1065984 | tf_op jit(solution)/shard_map/while/body/eval_jaxpr/convert_element_type | solution.py:38
  118.9 4.3 %multiply_convert_fusion.5 = (bf16[128,2048]{1,0:T(8,128)(2,1)S(1)}, bf16[128,2048]{1,0:T(8,128)(2,1)S(1)}) fusion(f32[128]{0:T(128)S(1)} %get-tuple-element.306, f32[2048]{0:T(1024)S(1)} %bitcast.118, f32[128]{0:T(128)S(1)} %get-tuple-element.308, f32[2048]{0:T(1024)S(1)} %bitcast.117), kind=kLoop, calls=%fused_computation.18.clone.1 | loop fusion | flops 2621440 | bytes 1065984 | tf_op jit(solution)/shard_map/while/body/eval_jaxpr/convert_element_type | solution.py:38
  125.7 4.3 %multiply_convert_fusion.5 = (bf16[128,2048]{1,0:T(8,128)(2,1)S(1)}, bf16[128,2048]{1,0:T(8,128)(2,1)S(1)}) fusion(f32[128]{0:T(128)S(1)} %get-tuple-element.306, f32[2048]{0:T(1024)S(1)} %bitcast.118, f32[128]{0:T(128)S(1)} %get-tuple-element.308, f32[2048]{0:T(1024)S(1)} %bitcast.117), kind=kLoop, calls=%fused_computation.18.clone.1 | loop fusion | flops 2621440 | bytes 1065984 | tf_op jit(solution)/shard_map/while/body/eval_jaxpr/convert_element_type | solution.py:38
  132.5 4.3 %multiply_convert_fusion.5 = (bf16[128,2048]{1,0:T(8,128)(2,1)S(1)}, bf16[128,2048]{1,0:T(8,128)(2,1)S(1)}) fusion(f32[128]{0:T(128)S(1)} %get-tuple-element.306, f32[2048]{0:T(1024)S(1)} %bitcast.118, f32[128]{0:T(128)S(1)} %get-tuple-element.308, f32[2048]{0:T(1024)S(1)} %bitcast.117), kind=kLoop, calls=%fused_computation.18.clone.1 | loop fusion | flops 2621440 | bytes 1065984 | tf_op jit(solution)/shard_map/while/body/eval_jaxpr/convert_element_type | solution.py:38
  139.3 4.3 %multiply_convert_fusion.5 = (bf16[128,2048]{1,0:T(8,128)(2,1)S(1)}, bf16[128,2048]{1,0:T(8,128)(2,1)S(1)}) fusion(f32[128]{0:T(128)S(1)} %get-tuple-element.306, f32[2048]{0:T(1024)S(1)} %bitcast.118, f32[128]{0:T(128)S(1)} %get-tuple-element.308, f32[2048]{0:T(1024)S(1)} %bitcast.117), kind=kLoop, calls=%fused_computation.18.clone.1 | loop fusion | flops 2621440 | bytes 1065984 | tf_op jit(solution)/shard_map/while/body/eval_jaxpr/convert_element_type | solution.py:38
  146.0 4.3 %multiply_convert_fusion.5 = (bf16[128,2048]{1,0:T(8,128)(2,1)S(1)}, bf16[128,2048]{1,0:T(8,128)(2,1)S(1)}) fusion(f32[128]{0:T(128)S(1)} %get-tuple-element.306, f32[2048]{0:T(1024)S(1)} %bitcast.118, f32[128]{0:T(128)S(1)} %get-tuple-element.308, f32[2048]{0:T(1024)S(1)} %bitcast.117), kind=kLoop, calls=%fused_computation.18.clone.1 | loop fusion | flops 2621440 | bytes 1065984 | tf_op jit(solution)/shard_map/while/body/eval_jaxpr/convert_element_type | solution.py:38
  152.8 4.3 %multiply_convert_fusion.5 = (bf16[128,2048]{1,0:T(8,128)(2,1)S(1)}, bf16[128,2048]{1,0:T(8,128)(2,1)S(1)}) fusion(f32[128]{0:T(128)S(1)} %get-tuple-element.306, f32[2048]{0:T(1024)S(1)} %bitcast.118, f32[128]{0:T(128)S(1)} %get-tuple-element.308, f32[2048]{0:T(1024)S(1)} %bitcast.117), kind=kLoop, calls=%fused_computation.18.clone.1 | loop fusion | flops 2621440 | bytes 1065984 | tf_op jit(solution)/shard_map/while/body/eval_jaxpr/convert_element_type | solution.py:38
  159.3 8.5 %copy.24 = f32[2,128,2048]{1,0,2:T(2,128)} copy(f32[2,128,2048]{1,2,0:T(8,128)S(1)} %get-tuple-element.162) | data formatting | bytes 4194304 | tf_op jit(solution)/shard_map/while | solution.py:84
  169.4 13.4 %collective-permute-start.1 = (f32[2,128,64]{2,1,0:T(8,128)S(1)}, f32[2,128,64]{2,1,0:T(8,128)S(1)}, u32[]{:S(2)}, u32[]{:S(2)}) collective-permute-start(f32[2,128,64]{2,1,0:T(8,128)S(1)} %select_bitcast_fusion.1), channel_id=1, source_target_pairs={{0,1},{1,2},{2,3},{3,4},{4,5},{5,6},{6,7},{7,8},{8,9},{9,10},{10,1... | collective-permute-start | bytes 196616 | tf_op jit(solution)/shard_map/ppermute | solution.py:25
  183.6 2.7 collective-permute-start.2
  187.6 3.8 %collective-permute-done.2 = f32[2,128,64]{2,1,0:T(8,128)S(1)} collective-permute-done((f32[2,128,64]{2,1,0:T(8,128)S(1)}, f32[2,128,64]{2,1,0:T(8,128)S(1)}, u32[]{:S(2)}, u32[]{:S(2)}) %collective-permute-start.2) | collective-permute-done | bytes 65568 | tf_op jit(solution)/shard_map/ppermute | solution.py:27
  196.9 129.8 %all-reduce.3.cloned.1.call-done = f32[2,128,2048]{1,0,2:T(2,128)} async-done(((f32[2,128,2048]{1,0,2:T(2,128)}), f32[2,128,2048]{1,0,2:T(2,128)}) %all-reduce.3.cloned.1.call-update) | async-done | bytes 2097168
  (188 shorter events, 44.7 us)
Async XLA Ops:
  7.8 36.3 %all-to-all-start = ((f32[16,2,128]{2,1,0:T(2,128)}), f32[16,2,128]{2,1,0:T(2,128)S(1)}, u32[]{:S(2)}, u32[]{:S(2)}) async-start(f32[16,2,128]{2,1,0:T(2,128)} %stack.63), calls=%async_computation | async-start | bytes 32768 | tf_op jit(solution)/shard_map/all_to_all | solution.py:65
  18.0 308.7 %all-reduce.3.cloned.1.call-start = ((), (), s32[]{:S(2)}) async-start(), calls=%async_computation.1 | async-start | bytes 4194304
  52.9 5.7 %collective-permute-start = (bf16[2,128,128]{2,1,0:T(8,128)(2,1)S(1)}, bf16[2,128,128]{2,1,0:T(8,128)(2,1)S(1)}, u32[]{:S(2)}, u32[]{:S(2)}) collective-permute-start(bf16[2,128,128]{2,1,0:T(8,128)(2,1)S(1)} %get-tuple-element.328), channel_id=1, source_target_pairs={{0,16},{16,32},{32,48},{48,64},{64,80},{80,96},{96,112},{112,128},... | collective-permute-start | bytes 196616 | tf_op jit(solution)/shard_map/while/body/eval_jaxpr/ppermute | solution.py:14
  60.0 5.9 %collective-permute-start = (bf16[2,128,128]{2,1,0:T(8,128)(2,1)S(1)}, bf16[2,128,128]{2,1,0:T(8,128)(2,1)S(1)}, u32[]{:S(2)}, u32[]{:S(2)}) collective-permute-start(bf16[2,128,128]{2,1,0:T(8,128)(2,1)S(1)} %get-tuple-element.328), channel_id=1, source_target_pairs={{0,16},{16,32},{32,48},{48,64},{64,80},{80,96},{96,112},{112,128},... | collective-permute-start | bytes 196616 | tf_op jit(solution)/shard_map/while/body/eval_jaxpr/ppermute | solution.py:14
  67.4 5.3 %collective-permute-start = (bf16[2,128,128]{2,1,0:T(8,128)(2,1)S(1)}, bf16[2,128,128]{2,1,0:T(8,128)(2,1)S(1)}, u32[]{:S(2)}, u32[]{:S(2)}) collective-permute-start(bf16[2,128,128]{2,1,0:T(8,128)(2,1)S(1)} %get-tuple-element.328), channel_id=1, source_target_pairs={{0,16},{16,32},{32,48},{48,64},{64,80},{80,96},{96,112},{112,128},... | collective-permute-start | bytes 196616 | tf_op jit(solution)/shard_map/while/body/eval_jaxpr/ppermute | solution.py:14
  74.1 5.9 %collective-permute-start = (bf16[2,128,128]{2,1,0:T(8,128)(2,1)S(1)}, bf16[2,128,128]{2,1,0:T(8,128)(2,1)S(1)}, u32[]{:S(2)}, u32[]{:S(2)}) collective-permute-start(bf16[2,128,128]{2,1,0:T(8,128)(2,1)S(1)} %get-tuple-element.328), channel_id=1, source_target_pairs={{0,16},{16,32},{32,48},{48,64},{64,80},{80,96},{96,112},{112,128},... | collective-permute-start | bytes 196616 | tf_op jit(solution)/shard_map/while/body/eval_jaxpr/ppermute | solution.py:14
  81.4 5.3 %collective-permute-start = (bf16[2,128,128]{2,1,0:T(8,128)(2,1)S(1)}, bf16[2,128,128]{2,1,0:T(8,128)(2,1)S(1)}, u32[]{:S(2)}, u32[]{:S(2)}) collective-permute-start(bf16[2,128,128]{2,1,0:T(8,128)(2,1)S(1)} %get-tuple-element.328), channel_id=1, source_target_pairs={{0,16},{16,32},{32,48},{48,64},{64,80},{80,96},{96,112},{112,128},... | collective-permute-start | bytes 196616 | tf_op jit(solution)/shard_map/while/body/eval_jaxpr/ppermute | solution.py:14
  88.2 5.9 %collective-permute-start = (bf16[2,128,128]{2,1,0:T(8,128)(2,1)S(1)}, bf16[2,128,128]{2,1,0:T(8,128)(2,1)S(1)}, u32[]{:S(2)}, u32[]{:S(2)}) collective-permute-start(bf16[2,128,128]{2,1,0:T(8,128)(2,1)S(1)} %get-tuple-element.328), channel_id=1, source_target_pairs={{0,16},{16,32},{32,48},{48,64},{64,80},{80,96},{96,112},{112,128},... | collective-permute-start | bytes 196616 | tf_op jit(solution)/shard_map/while/body/eval_jaxpr/ppermute | solution.py:14
  95.5 5.3 %collective-permute-start = (bf16[2,128,128]{2,1,0:T(8,128)(2,1)S(1)}, bf16[2,128,128]{2,1,0:T(8,128)(2,1)S(1)}, u32[]{:S(2)}, u32[]{:S(2)}) collective-permute-start(bf16[2,128,128]{2,1,0:T(8,128)(2,1)S(1)} %get-tuple-element.328), channel_id=1, source_target_pairs={{0,16},{16,32},{32,48},{48,64},{64,80},{80,96},{96,112},{112,128},... | collective-permute-start | bytes 196616 | tf_op jit(solution)/shard_map/while/body/eval_jaxpr/ppermute | solution.py:14
  102.3 7.1 %collective-permute-start = (bf16[2,128,128]{2,1,0:T(8,128)(2,1)S(1)}, bf16[2,128,128]{2,1,0:T(8,128)(2,1)S(1)}, u32[]{:S(2)}, u32[]{:S(2)}) collective-permute-start(bf16[2,128,128]{2,1,0:T(8,128)(2,1)S(1)} %get-tuple-element.328), channel_id=1, source_target_pairs={{0,16},{16,32},{32,48},{48,64},{64,80},{80,96},{96,112},{112,128},... | collective-permute-start | bytes 196616 | tf_op jit(solution)/shard_map/while/body/eval_jaxpr/ppermute | solution.py:14
  110.8 5.7 %collective-permute-start = (bf16[2,128,128]{2,1,0:T(8,128)(2,1)S(1)}, bf16[2,128,128]{2,1,0:T(8,128)(2,1)S(1)}, u32[]{:S(2)}, u32[]{:S(2)}) collective-permute-start(bf16[2,128,128]{2,1,0:T(8,128)(2,1)S(1)} %get-tuple-element.328), channel_id=1, source_target_pairs={{0,16},{16,32},{32,48},{48,64},{64,80},{80,96},{96,112},{112,128},... | collective-permute-start | bytes 196616 | tf_op jit(solution)/shard_map/while/body/eval_jaxpr/ppermute | solution.py:14
  117.9 5.3 %collective-permute-start = (bf16[2,128,128]{2,1,0:T(8,128)(2,1)S(1)}, bf16[2,128,128]{2,1,0:T(8,128)(2,1)S(1)}, u32[]{:S(2)}, u32[]{:S(2)}) collective-permute-start(bf16[2,128,128]{2,1,0:T(8,128)(2,1)S(1)} %get-tuple-element.328), channel_id=1, source_target_pairs={{0,16},{16,32},{32,48},{48,64},{64,80},{80,96},{96,112},{112,128},... | collective-permute-start | bytes 196616 | tf_op jit(solution)/shard_map/while/body/eval_jaxpr/ppermute | solution.py:14
  124.7 6.3 %collective-permute-start = (bf16[2,128,128]{2,1,0:T(8,128)(2,1)S(1)}, bf16[2,128,128]{2,1,0:T(8,128)(2,1)S(1)}, u32[]{:S(2)}, u32[]{:S(2)}) collective-permute-start(bf16[2,128,128]{2,1,0:T(8,128)(2,1)S(1)} %get-tuple-element.328), channel_id=1, source_target_pairs={{0,16},{16,32},{32,48},{48,64},{64,80},{80,96},{96,112},{112,128},... | collective-permute-start | bytes 196616 | tf_op jit(solution)/shard_map/while/body/eval_jaxpr/ppermute | solution.py:14
  132.4 5.3 %collective-permute-start = (bf16[2,128,128]{2,1,0:T(8,128)(2,1)S(1)}, bf16[2,128,128]{2,1,0:T(8,128)(2,1)S(1)}, u32[]{:S(2)}, u32[]{:S(2)}) collective-permute-start(bf16[2,128,128]{2,1,0:T(8,128)(2,1)S(1)} %get-tuple-element.328), channel_id=1, source_target_pairs={{0,16},{16,32},{32,48},{48,64},{64,80},{80,96},{96,112},{112,128},... | collective-permute-start | bytes 196616 | tf_op jit(solution)/shard_map/while/body/eval_jaxpr/ppermute | solution.py:14
  139.1 5.3 %collective-permute-start = (bf16[2,128,128]{2,1,0:T(8,128)(2,1)S(1)}, bf16[2,128,128]{2,1,0:T(8,128)(2,1)S(1)}, u32[]{:S(2)}, u32[]{:S(2)}) collective-permute-start(bf16[2,128,128]{2,1,0:T(8,128)(2,1)S(1)} %get-tuple-element.328), channel_id=1, source_target_pairs={{0,16},{16,32},{32,48},{48,64},{64,80},{80,96},{96,112},{112,128},... | collective-permute-start | bytes 196616 | tf_op jit(solution)/shard_map/while/body/eval_jaxpr/ppermute | solution.py:14
  145.8 5.3 %collective-permute-start = (bf16[2,128,128]{2,1,0:T(8,128)(2,1)S(1)}, bf16[2,128,128]{2,1,0:T(8,128)(2,1)S(1)}, u32[]{:S(2)}, u32[]{:S(2)}) collective-permute-start(bf16[2,128,128]{2,1,0:T(8,128)(2,1)S(1)} %get-tuple-element.328), channel_id=1, source_target_pairs={{0,16},{16,32},{32,48},{48,64},{64,80},{80,96},{96,112},{112,128},... | collective-permute-start | bytes 196616 | tf_op jit(solution)/shard_map/while/body/eval_jaxpr/ppermute | solution.py:14
  152.6 5.3 %collective-permute-start = (bf16[2,128,128]{2,1,0:T(8,128)(2,1)S(1)}, bf16[2,128,128]{2,1,0:T(8,128)(2,1)S(1)}, u32[]{:S(2)}, u32[]{:S(2)}) collective-permute-start(bf16[2,128,128]{2,1,0:T(8,128)(2,1)S(1)} %get-tuple-element.328), channel_id=1, source_target_pairs={{0,16},{16,32},{32,48},{48,64},{64,80},{80,96},{96,112},{112,128},... | collective-permute-start | bytes 196616 | tf_op jit(solution)/shard_map/while/body/eval_jaxpr/ppermute | solution.py:14
  167.9 0.7 copy-start.2
  167.9 18.4 %copy-start.5 = (u32[256]{0:T(256)S(1)}, u32[256]{0:T(256)}, u32[]{:S(2)}) copy-start(u32[256]{0:T(256)} %constant.141) | copy-start | bytes 3076
  167.9 19.6 %copy-start.1 = (s32[6,128]{1,0:T(8,128)S(1)}, s32[6,128]{1,0:T(8,128)}, u32[]{:S(2)}) copy-start(s32[6,128]{1,0:T(8,128)} %param.20) | copy-start | bytes 9220
  167.9 19.7 %copy-start = (f32[6,128]{1,0:T(8,128)S(1)}, f32[6,128]{1,0:T(8,128)}, u32[]{:S(2)}) copy-start(f32[6,128]{1,0:T(8,128)} %param.19) | copy-start | bytes 9220
  169.4 18.3 %collective-permute-start.1 = (f32[2,128,64]{2,1,0:T(8,128)S(1)}, f32[2,128,64]{2,1,0:T(8,128)S(1)}, u32[]{:S(2)}, u32[]{:S(2)}) collective-permute-start(f32[2,128,64]{2,1,0:T(8,128)S(1)} %select_bitcast_fusion.1), channel_id=1, source_target_pairs={{0,1},{1,2},{2,3},{3,4},{4,5},{5,6},{6,7},{7,8},{8,9},{9,10},{10,1... | collective-permute-start | bytes 196616 | tf_op jit(solution)/shard_map/ppermute | solution.py:25
  183.6 7.8 %collective-permute-start.2 = (f32[2,128,64]{2,1,0:T(8,128)S(1)}, f32[2,128,64]{2,1,0:T(8,128)S(1)}, u32[]{:S(2)}, u32[]{:S(2)}) collective-permute-start(f32[2,128,64]{2,1,0:T(8,128)S(1)} %select_bitcast_fusion), channel_id=1, source_target_pairs={{1,0},{2,1},{3,2},{4,3},{5,4},{6,5},{7,6},{8,7},{9,8},{10,9},{11,1... | collective-permute-start | bytes 196616 | tf_op jit(solution)/shard_map/ppermute | solution.py:27
  192.5 135.5 %copy-start.3 = (f32[128]{0:T(128)S(1)}, f32[128]{0:T(128)}, u32[]{:S(2)}) copy-start(f32[128]{0:T(128)} %param.18) | copy-start | bytes 1540
  192.5 135.5 %copy-start.4 = (f32[128]{0:T(128)S(1)}, f32[128]{0:T(128)}, u32[]{:S(2)}) copy-start(f32[128]{0:T(128)} %param.17) | copy-start | bytes 1540
Sparse Core Ops, SparseCore 0:
  168.0 158.5 all-reduce.2
